TPU v7x, 32 devices: a whole 2x2x4 slice. The times are simulated.
32 devices in a mesh: item: 8 (over z, x), head: 4 (over y, core).
Axes of the slice: x: 2, y: 2, z: 4, core: 2. Of those that a mesh axis runs over, the one named last changes fastest.
Arguments:
- media: bfloat16 [32, 512, 1536], P('item', 'head'), may hold values from -6 to 6
- latents: bfloat16 [32, 64, 1536], P('item', 'head'), may hold values from -6 to 6
- cotangent: bfloat16 [32, 64, 1536], P('item', 'head'), may hold values from -6 to 6
- frame_counts: int32 [32], P('item'), may hold values from 1 to 8, as said below
- query_weight: bfloat16 [1536, 1536], P('item', 'head'), may hold values from -0.15625 to 0.15625
- key_weight: bfloat16 [1536, 1536], P('item', 'head'), may hold values from -0.15625 to 0.15625
- value_weight: bfloat16 [1536, 1536], P('item', 'head'), may hold values from -0.15625 to 0.15625
- output_weight: bfloat16 [1536, 1536], P('item', 'head'), may hold values from -2.5 to 2.5
- up_weight: bfloat16 [1536, 6144], P('item', 'head'), may hold values from -0.15625 to 0.15625
- down_weight: bfloat16 [1536, 6144], P('item', 'head'), may hold values from -0.078125 to 0.078125
- media_gain: bfloat16 [1536], P('item'), may hold values from 0.25 to 1.75
- media_bias: bfloat16 [1536], P('item'), may hold values from -3 to 3
- latent_gain: bfloat16 [1536], P('item'), may hold values from 0.25 to 1.75
- latent_bias: bfloat16 [1536], P('item'), may hold values from -3 to 3
- ffn_gain: bfloat16 [1536], P('item'), may hold values from 0.25 to 1.75
- ffn_bias: bfloat16 [1536], P('item'), may hold values from -3 to 3
- time_embed: bfloat16 [8, 1536], P(None, 'item'), may hold values from -3 to 3
Outputs:
- latents_out: bfloat16 [32, 64, 1536], P('item', 'head')
- latents_grad: float32 [32, 64, 1536], P('item', 'head')
- media_grad: float32 [32, 512, 1536], P('item', 'head')
- query_grad: float32 [1536, 1536], P('item', 'head')
- key_grad: float32 [1536, 1536], P('item', 'head')
- value_grad: float32 [1536, 1536], P('item', 'head')
- output_grad: float32 [1536, 1536], P('item', 'head')
- up_grad: float32 [1536, 6144], P('item', 'head')
- down_grad: float32 [1536, 6144], P('item', 'head')
- media_gain_grad: float32 [1536], P('item')
- media_bias_grad: float32 [1536], P('item')
- latent_gain_grad: float32 [1536], P('item')
- latent_bias_grad: float32 [1536], P('item')
- ffn_gain_grad: float32 [1536], P('item')
- ffn_bias_grad: float32 [1536], P('item')
- time_grad: float32 [8, 1536], P(None, 'item')
Inputs may be any that keep to these rules, and one draw needn't show every extreme that they name: `frame_counts`: an item's true frame count; single images have 1, and some item in every draw has all 8.
All inputs are finite; a program needn't handle non-finite values.
Results may differ from a plain program's by a relative error of at most 0.02.
Values may be sent and summed in bfloat16 or wider, within the bound.
A program may use at most 88 MiB of HBM per device.

v0:
```python
import jax
import jax.numpy as jnp
from jax import lax
from jax.sharding import PartitionSpec as P

HEAD_DIM = 96
P_SIZE = 64


eps = 1e-05


def norm_forward(rows, gain, bias):
    row_mean = jnp.mean(rows, axis=-1, keepdims=True)
    centered = rows - row_mean
    variance = jnp.mean(centered * centered, axis=-1, keepdims=True)
    inverse = lax.rsqrt(variance + eps)
    normed = centered * inverse
    return (normed * gain + bias, normed, inverse)


def norm_backward(upstream, normed, inverse, gain):
    scaled = upstream * gain
    first_mean = jnp.mean(scaled, axis=-1, keepdims=True)
    second_mean = jnp.mean(scaled * normed, axis=-1, keepdims=True)
    return (
        inverse * (scaled - first_mean - normed * second_mean),
        jnp.sum(upstream * normed, axis=0),
        jnp.sum(upstream, axis=0),
    )


def times_transposed(left, right):
    return lax.dot_general(
        left, right, (((1,), (1,)), ((), ())), preferred_element_type=jnp.float32
    )


def transposed_times(left, right):
    return lax.dot_general(
        left, right, (((0,), (0,)), ((), ())), preferred_element_type=jnp.float32
    )


def micro_step(params, media_block, latent_block, cot_block, count, head_place):
    (
        w_query,
        w_key,
        w_value,
        w_output,
        w_up,
        w_down,
        g_media,
        b_media,
        g_latent,
        b_latent,
        g_ffn,
        b_ffn,
        time_table,
    ) = params
    local_media = media_block.shape[0]
    local_frames = local_media // P_SIZE
    local_heads = w_query.shape[1] // HEAD_DIM
    attn_scale = HEAD_DIM ** (-0.5)
    gain_media = g_media.astype(jnp.float32)
    gain_latent = g_latent.astype(jnp.float32)
    gain_ffn = g_ffn.astype(jnp.float32)
    time_rows = lax.dynamic_slice_in_dim(
        time_table.astype(jnp.float32), head_place * local_frames, local_frames, 0
    )
    shifted = (
        media_block.astype(jnp.float32).reshape(local_frames, P_SIZE, -1) + time_rows[:, None, :]
    ).reshape(local_media, -1)
    media_norm, media_hat, media_inv = norm_forward(
        shifted, gain_media, b_media.astype(jnp.float32)
    )
    latent_f = latent_block.astype(jnp.float32)
    latent_norm, latent_hat, latent_inv = norm_forward(
        latent_f, gain_latent, b_latent.astype(jnp.float32)
    )
    media_all, latent_all = (
        lax.all_gather(media_norm.astype(jnp.bfloat16), "head", axis=0, tiled=True),
        lax.all_gather(latent_norm.astype(jnp.bfloat16), "head", axis=0, tiled=True),
    )
    media_count = media_all.shape[0]
    latent_count = latent_all.shape[0]
    joined = jnp.concatenate([media_all, latent_all], axis=0)
    key_count = joined.shape[0]
    query = (attn_scale * jnp.dot(latent_all, w_query, preferred_element_type=jnp.float32)).astype(
        jnp.bfloat16
    )
    keys = jnp.dot(joined, w_key, preferred_element_type=jnp.float32).astype(jnp.bfloat16)
    values = jnp.dot(joined, w_value, preferred_element_type=jnp.float32).astype(jnp.bfloat16)
    query_heads = query.reshape(latent_count, local_heads, HEAD_DIM)
    key_heads = keys.reshape(key_count, local_heads, HEAD_DIM)
    value_heads = values.reshape(key_count, local_heads, HEAD_DIM)
    key_index = jnp.arange(key_count, dtype=jnp.int32)
    key_valid = (key_index // P_SIZE < count) | (key_index >= media_count)
    scores = jnp.einsum("lhe,nhe->hln", query_heads, key_heads, preferred_element_type=jnp.float32)
    scores = jnp.where(key_valid[None, None, :], scores, -1e30)
    row_peak = jnp.max(scores, axis=-1, keepdims=True)
    expo = jnp.exp(scores - row_peak)
    row_total = jnp.sum(expo, axis=-1, keepdims=True)
    log_total = row_peak + jnp.log(row_total)
    weights_low = (expo / row_total).astype(jnp.bfloat16)
    mixed = (
        jnp.einsum("hln,nhe->lhe", weights_low, value_heads, preferred_element_type=jnp.float32)
        .reshape(latent_count, -1)
        .astype(jnp.bfloat16)
    )
    attn_local = lax.psum_scatter(
        times_transposed(mixed, w_output).astype(jnp.bfloat16),
        "head",
        scatter_dimension=0,
        tiled=True,
    ).astype(jnp.float32)
    middle = latent_f + attn_local
    ffn_norm, ffn_hat, ffn_inv = norm_forward(middle, gain_ffn, b_ffn.astype(jnp.float32))
    ffn_all = lax.all_gather(ffn_norm.astype(jnp.bfloat16), "head", axis=0, tiled=True)
    pre_act = jnp.dot(ffn_all, w_up, preferred_element_type=jnp.float32)
    activated = jax.nn.gelu(pre_act).astype(jnp.bfloat16)
    ffn_local = lax.psum_scatter(
        times_transposed(activated, w_down).astype(jnp.bfloat16),
        "head",
        scatter_dimension=0,
        tiled=True,
    ).astype(jnp.float32)
    output = (middle + ffn_local).astype(jnp.bfloat16)
    upstream_all = lax.all_gather(cot_block, "head", axis=0, tiled=True)
    grad_down = transposed_times(upstream_all, activated)
    grad_act = jnp.dot(upstream_all, w_down, preferred_element_type=jnp.float32)
    grad_pre = jax.vjp(jax.nn.gelu, pre_act)[1](grad_act)[0].astype(jnp.bfloat16)
    grad_up = transposed_times(ffn_all, grad_pre)
    grad_ffn_norm = lax.psum_scatter(
        times_transposed(grad_pre, w_up).astype(jnp.bfloat16),
        "head",
        scatter_dimension=0,
        tiled=True,
    ).astype(jnp.float32)
    grad_mid_norm, grad_fgain, grad_fbias = norm_backward(grad_ffn_norm, ffn_hat, ffn_inv, gain_ffn)
    grad_middle = cot_block.astype(jnp.float32) + grad_mid_norm
    attended_grad = lax.all_gather(grad_middle.astype(jnp.bfloat16), "head", axis=0, tiled=True)
    grad_output = transposed_times(attended_grad, mixed)
    grad_mixed = jnp.dot(attended_grad, w_output, preferred_element_type=jnp.float32).astype(
        jnp.bfloat16
    )
    grad_mixed_heads = grad_mixed.reshape(latent_count, local_heads, HEAD_DIM)
    again = jnp.einsum("lhe,nhe->hln", query_heads, key_heads, preferred_element_type=jnp.float32)
    weights_again = jnp.where(key_valid[None, None, :], jnp.exp(again - log_total), 0.0)
    grad_values = (
        jnp.einsum(
            "hln,lhe->nhe",
            weights_again.astype(jnp.bfloat16),
            grad_mixed_heads,
            preferred_element_type=jnp.float32,
        )
        .astype(jnp.bfloat16)
        .reshape(key_count, -1)
    )
    grad_weights = jnp.einsum(
        "lhe,nhe->hln", grad_mixed_heads, value_heads, preferred_element_type=jnp.float32
    )
    row_inner = jnp.sum(weights_again * grad_weights, axis=-1, keepdims=True)
    grad_scores = (weights_again * (grad_weights - row_inner)).astype(jnp.bfloat16)
    grad_query = (
        jnp.einsum("hln,nhe->lhe", grad_scores, key_heads, preferred_element_type=jnp.float32)
        .astype(jnp.bfloat16)
        .reshape(latent_count, -1)
    )
    grad_keys = (
        jnp.einsum("hln,lhe->nhe", grad_scores, query_heads, preferred_element_type=jnp.float32)
        .astype(jnp.bfloat16)
        .reshape(key_count, -1)
    )
    grad_wquery = attn_scale * transposed_times(latent_all, grad_query)
    grad_wkey = transposed_times(joined, grad_keys)
    grad_wvalue = transposed_times(joined, grad_values)
    grad_joined = times_transposed(grad_keys, w_key) + times_transposed(grad_values, w_value)
    grad_latent_all = grad_joined[media_count:] + attn_scale * times_transposed(grad_query, w_query)
    media_back, latent_back = (
        lax.psum_scatter(
            grad_joined[:media_count].astype(jnp.bfloat16), "head", scatter_dimension=0, tiled=True
        ).astype(jnp.float32),
        lax.psum_scatter(
            grad_latent_all.astype(jnp.bfloat16), "head", scatter_dimension=0, tiled=True
        ).astype(jnp.float32),
    )
    grad_shifted, grad_mgain, grad_mbias = norm_backward(
        media_back, media_hat, media_inv, gain_media
    )
    time_local = jnp.sum(grad_shifted.reshape(local_frames, P_SIZE, -1), axis=1)
    grad_time = lax.dynamic_update_slice_in_dim(
        jnp.zeros(time_table.shape, jnp.float32), time_local, head_place * local_frames, 0
    )
    grad_lat_norm, grad_lgain, grad_lbias = norm_backward(
        latent_back, latent_hat, latent_inv, gain_latent
    )
    grad_latent = grad_middle + grad_lat_norm
    grads = (
        grad_wquery,
        grad_wkey,
        grad_wvalue,
        grad_output,
        grad_up,
        grad_down,
        grad_mgain,
        grad_mbias,
        grad_lgain,
        grad_lbias,
        grad_fgain,
        grad_fbias,
        grad_time,
    )
    return (output, grad_latent, grad_shifted, grads)


def on_device(
    media,
    latents,
    cotangent,
    frame_counts,
    query_weight,
    key_weight,
    value_weight,
    output_weight,
    up_weight,
    down_weight,
    media_gain,
    media_bias,
    latent_gain,
    latent_bias,
    ffn_gain,
    ffn_bias,
    time_embed,
):
    micro_count = media.shape[0]
    head_place = lax.axis_index("head")
    outputs = []
    latent_grads = []
    media_grads = []
    running = None
    for micro_index in range(micro_count):
        params = (
            lax.all_gather(query_weight, "item", axis=0, tiled=True),
            lax.all_gather(key_weight, "item", axis=0, tiled=True),
            lax.all_gather(value_weight, "item", axis=0, tiled=True),
            lax.all_gather(output_weight, "item", axis=0, tiled=True),
            lax.all_gather(up_weight, "item", axis=0, tiled=True),
            lax.all_gather(down_weight, "item", axis=0, tiled=True),
            lax.all_gather(media_gain, "item", axis=0, tiled=True),
            lax.all_gather(media_bias, "item", axis=0, tiled=True),
            lax.all_gather(latent_gain, "item", axis=0, tiled=True),
            lax.all_gather(latent_bias, "item", axis=0, tiled=True),
            lax.all_gather(ffn_gain, "item", axis=0, tiled=True),
            lax.all_gather(ffn_bias, "item", axis=0, tiled=True),
            lax.all_gather(time_embed, "item", axis=1, tiled=True),
        )
        output, grad_latent, grad_media, grads = micro_step(
            params,
            media[micro_index],
            latents[micro_index],
            cotangent[micro_index],
            frame_counts[micro_index],
            head_place,
        )
        outputs.append(output)
        latent_grads.append(grad_latent)
        media_grads.append(grad_media)
        (
            sum_query,
            sum_key,
            sum_value,
            sum_output,
            sum_up,
            sum_down,
            sum_mgain,
            sum_mbias,
            sum_lgain,
            sum_lbias,
            sum_fgain,
            sum_fbias,
            sum_time,
        ) = grads
        portion = (
            lax.psum_scatter(sum_query, "item", scatter_dimension=0, tiled=True),
            lax.psum_scatter(sum_key, "item", scatter_dimension=0, tiled=True),
            lax.psum_scatter(sum_value, "item", scatter_dimension=0, tiled=True),
            lax.psum_scatter(sum_output, "item", scatter_dimension=0, tiled=True),
            lax.psum_scatter(sum_up, "item", scatter_dimension=0, tiled=True),
            lax.psum_scatter(sum_down, "item", scatter_dimension=0, tiled=True),
            lax.psum_scatter(
                lax.psum(sum_mgain.astype(jnp.bfloat16), "head").astype(jnp.float32),
                "item",
                scatter_dimension=0,
                tiled=True,
            ),
            lax.psum_scatter(
                lax.psum(sum_mbias.astype(jnp.bfloat16), "head").astype(jnp.float32),
                "item",
                scatter_dimension=0,
                tiled=True,
            ),
            lax.psum_scatter(
                lax.psum(sum_lgain.astype(jnp.bfloat16), "head").astype(jnp.float32),
                "item",
                scatter_dimension=0,
                tiled=True,
            ),
            lax.psum_scatter(
                lax.psum(sum_lbias.astype(jnp.bfloat16), "head").astype(jnp.float32),
                "item",
                scatter_dimension=0,
                tiled=True,
            ),
            lax.psum_scatter(
                lax.psum(sum_fgain.astype(jnp.bfloat16), "head").astype(jnp.float32),
                "item",
                scatter_dimension=0,
                tiled=True,
            ),
            lax.psum_scatter(
                lax.psum(sum_fbias.astype(jnp.bfloat16), "head").astype(jnp.float32),
                "item",
                scatter_dimension=0,
                tiled=True,
            ),
            lax.psum_scatter(
                lax.psum(sum_time.astype(jnp.bfloat16), "head").astype(jnp.float32),
                "item",
                scatter_dimension=1,
                tiled=True,
            ),
        )
        running = portion if running is None else jax.tree.map(jnp.add, running, portion)
    return (
        jnp.stack(outputs),
        jnp.stack(latent_grads),
        jnp.stack(media_grads),
        running[0],
        running[1],
        running[2],
        running[3],
        running[4],
        running[5],
        running[6],
        running[7],
        running[8],
        running[9],
        running[10],
        running[11],
        running[12],
    )


def solution(mesh):
    placed = (
        P("item", "head", None),
        P("item", "head", None),
        P("item", "head", None),
        P("item"),
        P("item", "head"),
        P("item", "head"),
        P("item", "head"),
        P("item", "head"),
        P("item", "head"),
        P("item", "head"),
        P("item"),
        P("item"),
        P("item"),
        P("item"),
        P("item"),
        P("item"),
        P(None, "item"),
    )
    return jax.shard_map(
        on_device,
        mesh=mesh,
        in_specs=placed,
        out_specs=(
            P("item", "head", None),
            P("item", "head", None),
            P("item", "head", None),
            P("item", "head"),
            P("item", "head"),
            P("item", "head"),
            P("item", "head"),
            P("item", "head"),
            P("item", "head"),
            P("item"),
            P("item"),
            P("item"),
            P("item"),
            P("item"),
            P("item"),
            P(None, "item"),
        ),
        check_vma=False,
    )
```

profile of v0, /device:TPU:0, one launch (start us, length us, event | category | flops | bytes accessed | tf_op | source)
XLA Modules:
  0.0 1761.3 jit_solution(5666927556839195206)
XLA Ops:
  15.2 39.1 %all-reduce.13 = (bf16[1536]{0:T(1024)(128)(2,1)S(1)}, bf16[1536]{0:T(1024)(128)(2,1)S(1)}, bf16[1536]{0:T(1024)(128)(2,1)S(1)}, bf16[1536]{0:T(1024)(128)(2,1)S...) all-reduce(bf16[1536]{0:T(1024)(128)(2,1)S(1)} %dynamic-update-slic, ...), channel_id=1, replica_groups=mesh['item'=8,'head'=4] {'item'}, use_global_device_ids=true, to_apply=%add.5 | all-reduce | flops 9216 | bytes 36864
  54.3 30.5 %all-gather.4 = bf16[8,192,8]{1,2,0:T(8,128)(2,1)S(1)} all-gather(bf16[1,192,8]{1,2,0:T(8,128)(2,1)} %bitcast.780), channel_id=1, replica_groups=mesh['item'=8,'head'=4] {'item'}, dimensions={0}, use_global_device_ids=true | all-gather | bytes 27648 | tf_op jit(solution)/shard_map/all_gather | solution.py:256
  96.1 6.9 all_gather.158
  109.5 41.2 %all-gather.22.cloned.1.call-done = bf16[1536,384]{1,0:T(8,128)(2,1)} async-done(((bf16[192,384]{1,0:T(8,128)(2,1)}), bf16[1536,384]{1,0:T(8,128)(2,1)}) %all-gather.22.cloned.1.call-update) | async-done | bytes 1179664 | tf_op jit(solution)/shard_map/all_gather | solution.py:245
  153.3 39.3 %all-gather.18.cloned.1.call-done = bf16[1536,384]{1,0:T(8,128)(2,1)} async-done(((bf16[192,384]{1,0:T(8,128)(2,1)}), bf16[1536,384]{1,0:T(8,128)(2,1)}) %all-gather.18.cloned.1.call-update) | async-done | bytes 1179664 | tf_op jit(solution)/shard_map/all_gather | solution.py:246
  198.4 36.1 %all-gather.24.cloned.1.call-done = bf16[1536,384]{1,0:T(8,128)(2,1)} async-done(((bf16[192,384]{1,0:T(8,128)(2,1)}), bf16[1536,384]{1,0:T(8,128)(2,1)}) %all-gather.24.cloned.1.call-update) | async-done | bytes 1179664 | tf_op jit(solution)/shard_map/all_gather | solution.py:247
  238.4 6.1 all-gather.1
  244.4 7.4 all-gather
  251.8 6.0 all-gather.3
  257.8 6.0 all-gather.2
  270.8 8.1 all-gather.30.cloned.1.call-done
  281.6 19.1 %all-gather.34.cloned.1.call-done = bf16[512,1536]{1,0:T(8,128)(2,1)} async-done(((bf16[128,1536]{1,0:T(8,128)(2,1)}), bf16[512,1536]{1,0:T(8,128)(2,1)}) %all-gather.34.cloned.1.call-update) | async-done | bytes 1572880 | tf_op jit(solution)/shard_map/all_gather | solution.py:82
  303.4 20.1 %reduce-scatter.40.cloned.1.call-done = bf16[16,1536]{1,0:T(8,128)(2,1)} async-done(((bf16[64,1536]{1,0:T(8,128)(2,1)}), bf16[16,1536]{1,0:T(8,128)(2,1)}) %reduce-scatter.40.cloned.1.call-update) | async-done | bytes 49168 | tf_op jit(solution)/shard_map/reduce_scatter | solution.py:111
  327.2 5.6 all_gather.161
  333.2 5.6 all_gather.155
  339.9 6.1 all_gather.144
  347.1 3.8 convolution_convert_fusion.26
  391.4 6.4 all_gather.159
  399.0 6.4 all-gather.26.cloned.1.call-done
  405.4 4.1 fusion.335
  409.5 76.2 %all-gather.28.cloned.1.call-done = bf16[1536,1536]{1,0:T(8,128)(2,1)} async-done(((bf16[192,1536]{1,0:T(8,128)(2,1)}), bf16[1536,1536]{1,0:T(8,128)(2,1)}) %all-gather.28.cloned.1.call-update) | async-done | bytes 4718608 | tf_op jit(solution)/shard_map/all_gather | solution.py:249
  485.7 3.7 fusion.118
  493.5 13.0 reduce-scatter.44.cloned.1.call-done
  506.5 22.8 %reduce-scatter.36.cloned.1.call-done = bf16[16,1536]{1,0:T(8,128)(2,1)} async-done(((bf16[64,1536]{1,0:T(8,128)(2,1)}), bf16[16,1536]{1,0:T(8,128)(2,1)}) %reduce-scatter.36.cloned.1.call-update) | async-done | bytes 49168 | tf_op jit(solution)/shard_map/reduce_scatter | solution.py:111
  529.3 22.6 %reduce-scatter.32.cloned.1.call-done = bf16[16,1536]{1,0:T(8,128)(2,1)} async-done(((bf16[64,1536]{1,0:T(8,128)(2,1)}), bf16[16,1536]{1,0:T(8,128)(2,1)}) %reduce-scatter.32.cloned.1.call-update) | async-done | bytes 49168 | tf_op jit(solution)/shard_map/reduce_scatter | solution.py:111
  551.9 22.6 %reduce-scatter.56.cloned.1.call-done = bf16[16,1536]{1,0:T(8,128)(2,1)} async-done(((bf16[64,1536]{1,0:T(8,128)(2,1)}), bf16[16,1536]{1,0:T(8,128)(2,1)}) %reduce-scatter.56.cloned.1.call-update) | async-done | bytes 49168 | tf_op jit(solution)/shard_map/reduce_scatter | solution.py:134
  577.1 5.8 all_gather.168
  597.7 19.8 %reduce-scatter.58.cloned.1.call-done = bf16[16,1536]{1,0:T(8,128)(2,1)} async-done(((bf16[64,1536]{1,0:T(8,128)(2,1)}), bf16[16,1536]{1,0:T(8,128)(2,1)}) %reduce-scatter.58.cloned.1.call-update) | async-done | bytes 49168 | tf_op jit(solution)/shard_map/reduce_scatter | solution.py:184
  620.9 6.0 all_gather.156
  627.0 5.6 all_gather.162
  646.5 3.6 fusion.111
  650.2 6.1 all_gather.151
  656.2 4.6 convolution_convert_fusion.2
  660.9 3.4 fusion.333
  669.1 4.6 convolution_convert_fusion.3
  674.6 4.7 convolution_convert_fusion.4
  679.4 6.2 reduce-scatter.52.cloned.1.call-done
  685.6 22.8 %reduce-scatter.48.cloned.1.call-done = bf16[16,1536]{1,0:T(8,128)(2,1)} async-done(((bf16[64,1536]{1,0:T(8,128)(2,1)}), bf16[16,1536]{1,0:T(8,128)(2,1)}) %reduce-scatter.48.cloned.1.call-update) | async-done | bytes 49168 | tf_op jit(solution)/shard_map/reduce_scatter | solution.py:134
  712.7 5.6 all_gather.164
  727.3 3.7 reduce-scatter.46.cloned.1.call-done
  732.7 5.6 all_gather.166
  745.3 5.6 all_gather.170
  799.5 6.4 reduce-scatter.54.cloned.1.call-done
  807.3 21.4 %reduce-scatter.50.cloned.1.call-done = bf16[16,1536]{1,0:T(8,128)(2,1)} async-done(((bf16[64,1536]{1,0:T(8,128)(2,1)}), bf16[16,1536]{1,0:T(8,128)(2,1)}) %reduce-scatter.50.cloned.1.call-update) | async-done | bytes 49168 | tf_op jit(solution)/shard_map/reduce_scatter | solution.py:184
  832.0 27.4 %reduce-scatter.68.cloned.1.call-done = bf16[128,1536]{1,0:T(8,128)(2,1)} async-done(((bf16[512,1536]{1,0:T(8,128)(2,1)}), bf16[128,1536]{1,0:T(8,128)(2,1)}) %reduce-scatter.68.cloned.1.call-update) | async-done | bytes 393232 | tf_op jit(solution)/shard_map/reduce_scatter | solution.py:181
  861.1 29.2 %reduce-scatter.70.cloned.1.call-done = bf16[128,1536]{1,0:T(8,128)(2,1)} async-done(((bf16[512,1536]{1,0:T(8,128)(2,1)}), bf16[128,1536]{1,0:T(8,128)(2,1)}) %reduce-scatter.70.cloned.1.call-update) | async-done | bytes 393232 | tf_op jit(solution)/shard_map/reduce_scatter | solution.py:181
  890.3 30.6 %reduce-scatter.66.cloned.1.call-done = bf16[128,1536]{1,0:T(8,128)(2,1)} async-done(((bf16[512,1536]{1,0:T(8,128)(2,1)}), bf16[128,1536]{1,0:T(8,128)(2,1)}) %reduce-scatter.66.cloned.1.call-update) | async-done | bytes 393232 | tf_op jit(solution)/shard_map/reduce_scatter | solution.py:181
  920.9 30.7 %reduce-scatter.64.cloned.1.call-done = bf16[128,1536]{1,0:T(8,128)(2,1)} async-done(((bf16[512,1536]{1,0:T(8,128)(2,1)}), bf16[128,1536]{1,0:T(8,128)(2,1)}) %reduce-scatter.64.cloned.1.call-update) | async-done | bytes 393232 | tf_op jit(solution)/shard_map/reduce_scatter | solution.py:181
  951.7 3.5 fusion.61
  963.4 4.6 convolution_convert_fusion.6
  968.1 4.6 convolution_convert_fusion.10
  972.8 4.6 convolution_convert_fusion.8
  979.8 19.5 %all-reduce.17.cloned.1.call-done = (bf16[1536]{0:T(1024)(128)(2,1)}, bf16[1536]{0:T(1024)(128)(2,1)}, bf16[1536]{0:T(1024)(128)(2,1)}, bf16[1536]{0:T(1024)(128...) async-done(((bf16[1536]{0:T(1024)(128)(2,1)}, ...) | async-done | bytes 172048 | tf_op jit(solution)/shard_map/psum | solution.py:292
  1033.5 5.1 fusion
  1038.6 9.6 copy.134
  1053.7 5.1 convolution_add_fusion.3
  1079.2 37.6 %all-reduce.12 = (f32[1536]{0:T(1024)S(1)}, f32[1536]{0:T(1024)S(1)}, f32[1536]{0:T(1024)S(1)}, f32[1536]{0:T(1024)S(1)}, f32[1536]{0:T(1024)S(1)}, /*index=5*/f32[1536]{0:T(1024)S(1)}) all-reduce(f32[1536]{0:T(1024)S(1)} %add_add_fusion.6, f32[1536]{0:T(1024)S(1)} %add_add_fusion.5, ...), channel_id=71, replica_groups=mesh['item'=8,'head'=4] {'item'}, use_global_device_ids=true, to_apply=%region_106.107.clone | all-reduce | flops 9216 | bytes 73728
  1120.6 12.3 reduce-scatter.84.cloned.1.call-done
  1134.5 70.4 %reduce-scatter.78.cloned.1.call-done = f32[192,384]{1,0:T(8,128)} async-done(((f32[1536,384]{1,0:T(8,128)}), f32[192,384]{1,0:T(8,128)}) %reduce-scatter.78.cloned.1.call-update) | async-done | bytes 294928 | tf_op jit(solution)/shard_map/reduce_scatter | solution.py:288
  1204.9 72.1 %reduce-scatter.72.cloned.1.call-done = f32[192,384]{1,0:T(8,128)} async-done(((f32[1536,384]{1,0:T(8,128)}), f32[192,384]{1,0:T(8,128)}) %reduce-scatter.72.cloned.1.call-update) | async-done | bytes 294928 | tf_op jit(solution)/shard_map/reduce_scatter | solution.py:285
  1277.0 72.2 %reduce-scatter.74.cloned.1.call-done = f32[192,384]{1,0:T(8,128)} async-done(((f32[1536,384]{1,0:T(8,128)}), f32[192,384]{1,0:T(8,128)}) %reduce-scatter.74.cloned.1.call-update) | async-done | bytes 294928 | tf_op jit(solution)/shard_map/reduce_scatter | solution.py:286
  1349.2 72.1 %reduce-scatter.76.cloned.1.call-done = f32[192,384]{1,0:T(8,128)} async-done(((f32[1536,384]{1,0:T(8,128)}), f32[192,384]{1,0:T(8,128)}) %reduce-scatter.76.cloned.1.call-update) | async-done | bytes 294928 | tf_op jit(solution)/shard_map/reduce_scatter | solution.py:287
  1421.3 166.4 %reduce-scatter.82.cloned.1.call-done = f32[192,1536]{1,0:T(8,128)} async-done(((f32[1536,1536]{1,0:T(8,128)}), f32[192,1536]{1,0:T(8,128)}) %reduce-scatter.82.cloned.1.call-update) | async-done | bytes 1179664
  1587.7 166.6 %reduce-scatter.80.cloned.1.call-done = f32[192,1536]{1,0:T(8,128)} async-done(((f32[1536,1536]{1,0:T(8,128)}), f32[192,1536]{1,0:T(8,128)}) %reduce-scatter.80.cloned.1.call-update) | async-done | bytes 1179664 | tf_op jit(solution)/shard_map/reduce_scatter | solution.py:289
  (881 shorter events, 291.4 us)
Async XLA Ops:
  7.2 95.9 %all-gather.20.cloned.1.call-start = ((), (), s32[]{:S(2)}) async-start(), calls=%async_computation.29 | async-start | bytes 1327104 | tf_op jit(solution)/shard_map/all_gather | solution.py:244
  7.9 100.0 %all-gather.32.cloned.1.call-start = ((), (), s32[]{:S(2)}) async-start(), calls=%async_computation.39 | async-start | bytes 1966080 | tf_op jit(solution)/shard_map/all_gather | solution.py:82
  11.7 75.2 %copy-start.3 = (bf16[4,128,1536]{2,1,0:T(8,128)(2,1)S(1)}, bf16[4,128,1536]{2,1,0:T(8,128)(2,1)}, u32[]{:S(2)}) copy-start(bf16[4,128,1536]{2,1,0:T(8,128)(2,1)} %param.17) | copy-start | bytes 4718596
  89.8 60.8 %all-gather.22.cloned.1.call-start = ((), (), s32[]{:S(2)}) async-start(), calls=%async_computation.30 | async-start | bytes 1327104 | tf_op jit(solution)/shard_map/all_gather | solution.py:245
  90.6 102.0 %all-gather.18.cloned.1.call-start = ((), (), s32[]{:S(2)}) async-start(), calls=%async_computation.28 | async-start | bytes 1327104 | tf_op jit(solution)/shard_map/all_gather | solution.py:246
  91.2 143.3 %all-gather.24.cloned.1.call-start = ((), (), s32[]{:S(2)}) async-start(), calls=%async_computation.31 | async-start | bytes 1327104 | tf_op jit(solution)/shard_map/all_gather | solution.py:247
  91.8 176.4 %all-gather.16.cloned.1.call-start = ((), (), s32[]{:S(2)}) async-start(), calls=%async_computation.27 | async-start | bytes 1966080 | tf_op jit(solution)/shard_map/all_gather | solution.py:82
  92.3 186.5 %all-gather.30.cloned.1.call-start = ((), (), s32[]{:S(2)}) async-start(), calls=%async_computation.36 | async-start | bytes 1966080 | tf_op jit(solution)/shard_map/all_gather | solution.py:82
  93.1 207.6 %all-gather.34.cloned.1.call-start = ((), (), s32[]{:S(2)}) async-start(), calls=%async_computation.42 | async-start | bytes 1966080 | tf_op jit(solution)/shard_map/all_gather | solution.py:82
  93.8 229.6 %reduce-scatter.40.cloned.1.call-start = ((), (), s32[]{:S(2)}) async-start(), calls=%async_computation.40 | async-start | bytes 245760 | tf_op jit(solution)/shard_map/reduce_scatter | solution.py:111
  95.2 102.4 %copy-start.163 = (pred[576]{0:T(1024)(128)(4,1)}, pred[576]{0:T(1024)(128)(4,1)S(1)}, u32[]{:S(2)}) copy-start(pred[576]{0:T(1024)(128)(4,1)S(1)} %fusion.310) | copy-start | bytes 1732
  104.7 92.2 %copy-start.118 = (bf16[64,4,96]{2,1,0:T(4,128)(2,1)}, bf16[64,4,96]{2,1,0:T(4,128)(2,1)S(1)}, u32[]{:S(2)}) copy-start(bf16[64,4,96]{2,1,0:T(4,128)(2,1)S(1)} %reshape.599) | copy-start | bytes 147460
  109.5 83.1 %copy-start.19 = (bf16[576,1536]{1,0:T(8,128)(2,1)}, bf16[576,1536]{1,0:T(8,128)(2,1)S(1)}, u32[]{:S(2)}) copy-start(bf16[576,1536]{1,0:T(8,128)(2,1)S(1)} %constant_dynamic-update-slice_fusion.4) | copy-start | bytes 5308420
  198.3 69.2 %copy-start.255 = (f32[16]{0:T(128)S(1)}, f32[16]{0:T(128)}, u32[]{:S(2)}) copy-start(f32[16]{0:T(128)} %get-tuple-element.125) | copy-start | bytes 196
  236.9 168.5 %all-gather.26.cloned.1.call-start = ((), (), s32[]{:S(2)}) async-start(), calls=%async_computation.33 | async-start | bytes 5308416 | tf_op jit(solution)/shard_map/all_gather | solution.py:248
  237.5 248.2 %all-gather.28.cloned.1.call-start = ((), (), s32[]{:S(2)}) async-start(), calls=%async_computation.34 | async-start | bytes 5308416 | tf_op jit(solution)/shard_map/all_gather | solution.py:249
  238.3 268.2 %reduce-scatter.44.cloned.1.call-start = ((), (), s32[]{:S(2)}) async-start(), calls=%async_computation.43 | async-start | bytes 245760 | tf_op jit(solution)/shard_map/reduce_scatter | solution.py:111
  238.3 87.3 %copy-start.148 = (f32[1536]{0:T(1024)}, f32[1536]{0:T(1024)S(1)}, u32[]{:S(2)}) copy-start(f32[1536]{0:T(1024)S(1)} %convert_element_type.688) | copy-start | bytes 18436
  381.5 147.8 %reduce-scatter.36.cloned.1.call-start = ((), (), s32[]{:S(2)}) async-start(), calls=%async_computation.37 | async-start | bytes 245760 | tf_op jit(solution)/shard_map/reduce_scatter | solution.py:111
  387.4 164.5 %reduce-scatter.32.cloned.1.call-start = ((), (), s32[]{:S(2)}) async-start(), calls=%async_computation.32 | async-start | bytes 245760 | tf_op jit(solution)/shard_map/reduce_scatter | solution.py:111
  398.9 175.6 %reduce-scatter.56.cloned.1.call-start = ((), (), s32[]{:S(2)}) async-start(), calls=%async_computation.49 | async-start | bytes 245760 | tf_op jit(solution)/shard_map/reduce_scatter | solution.py:134
  490.1 84.4 %copy-start.106 = (bf16[16,1536]{1,0:T(8,128)(2,1)S(1)}, bf16[16,1536]{1,0:T(8,128)(2,1)}, u32[]{:S(2)}) copy-start(bf16[16,1536]{1,0:T(8,128)(2,1)} %reduce-scatter.40.cloned.1.call-done) | copy-start | bytes 147460
  490.1 84.4 %copy-start.189 = (f32[16]{0:T(128)S(1)}, f32[16]{0:T(128)}, u32[]{:S(2)}) copy-start(f32[16]{0:T(128)} %copy-done.188) | copy-start | bytes 196
  490.1 84.4 %copy-start.205 = (f32[16]{0:T(128)S(1)}, f32[16]{0:T(128)}, u32[]{:S(2)}) copy-start(f32[16]{0:T(128)} %copy-done.204) | copy-start | bytes 196
  492.3 125.1 %reduce-scatter.58.cloned.1.call-start = ((), (), s32[]{:S(2)}) async-start(), calls=%async_computation.50 | async-start | bytes 245760 | tf_op jit(solution)/shard_map/reduce_scatter | solution.py:184
  597.6 81.8 %reduce-scatter.60.cloned.1.call-start = ((), (), s32[]{:S(2)}) async-start(), calls=%async_computation.51 | async-start | bytes 245760 | tf_op jit(solution)/shard_map/reduce_scatter | solution.py:134
  597.6 133.4 %copy-start.173 = (f32[16]{0:T(128)}, f32[16]{0:T(128)S(1)}, u32[]{:S(2)}) copy-start(f32[16]{0:T(128)S(1)} %broadcast_multiply_fusion.20) | copy-start | bytes 196
  597.7 133.4 %copy-start.171 = (f32[16]{0:T(128)}, f32[16]{0:T(128)S(1)}, u32[]{:S(2)}) copy-start(f32[16]{0:T(128)S(1)} %broadcast_multiply_fusion.16) | copy-start | bytes 196
  619.2 92.5 %copy-start.195 = (f32[16]{0:T(128)}, f32[16]{0:T(128)S(1)}, u32[]{:S(2)}) copy-start(f32[16]{0:T(128)S(1)} %add_rsqrt_fusion.9) | copy-start | bytes 196
  619.2 111.8 %copy-start.194 = (f32[16]{0:T(128)}, f32[16]{0:T(128)S(1)}, u32[]{:S(2)}) copy-start(f32[16]{0:T(128)S(1)} %add_rsqrt_fusion.6) | copy-start | bytes 196
  619.3 111.8 %copy-start.193 = (f32[16]{0:T(128)}, f32[16]{0:T(128)S(1)}, u32[]{:S(2)}) copy-start(f32[16]{0:T(128)S(1)} %add_rsqrt_fusion) | copy-start | bytes 196
  643.0 42.6 %reduce-scatter.52.cloned.1.call-start = ((), (), s32[]{:S(2)}) async-start(), calls=%async_computation.47 | async-start | bytes 245760 | tf_op jit(solution)/shard_map/reduce_scatter | solution.py:134
  660.8 47.6 %reduce-scatter.48.cloned.1.call-start = ((), (), s32[]{:S(2)}) async-start(), calls=%async_computation.45 | async-start | bytes 245760 | tf_op jit(solution)/shard_map/reduce_scatter | solution.py:134
  673.7 57.3 %reduce-scatter.46.cloned.1.call-start = ((), (), s32[]{:S(2)}) async-start(), calls=%async_computation.44 | async-start | bytes 245760 | tf_op jit(solution)/shard_map/reduce_scatter | solution.py:122
  679.4 118.7 %reduce-scatter.62.cloned.1.call-start = ((), (), s32[]{:S(2)}) async-start(), calls=%async_computation.52 | async-start | bytes 245760 | tf_op jit(solution)/shard_map/reduce_scatter | solution.py:184
  763.2 42.7 %reduce-scatter.54.cloned.1.call-start = ((), (), s32[]{:S(2)}) async-start(), calls=%async_computation.48 | async-start | bytes 245760 | tf_op jit(solution)/shard_map/reduce_scatter | solution.py:184
  772.7 56.0 %reduce-scatter.50.cloned.1.call-start = ((), (), s32[]{:S(2)}) async-start(), calls=%async_computation.46 | async-start | bytes 245760 | tf_op jit(solution)/shard_map/reduce_scatter | solution.py:184
  781.3 78.0 %reduce-scatter.68.cloned.1.call-start = ((), (), s32[]{:S(2)}) async-start(), calls=%async_computation.55 | async-start | bytes 1966080 | tf_op jit(solution)/shard_map/reduce_scatter | solution.py:181
  784.7 105.6 %reduce-scatter.70.cloned.1.call-start = ((), (), s32[]{:S(2)}) async-start(), calls=%async_computation.56 | async-start | bytes 1966080 | tf_op jit(solution)/shard_map/reduce_scatter | solution.py:181
  788.0 132.9 %reduce-scatter.66.cloned.1.call-start = ((), (), s32[]{:S(2)}) async-start(), calls=%async_computation.54 | async-start | bytes 1966080 | tf_op jit(solution)/shard_map/reduce_scatter | solution.py:181
  791.3 160.3 %reduce-scatter.64.cloned.1.call-start = ((), (), s32[]{:S(2)}) async-start(), calls=%async_computation.53 | async-start | bytes 1966080 | tf_op jit(solution)/shard_map/reduce_scatter | solution.py:181
  794.8 156.9 %copy-start.4 = (bf16[4,128,1536]{2,1,0:T(8,128)(2,1)S(1)}, bf16[4,128,1536]{2,1,0:T(8,128)(2,1)}, u32[]{:S(2)}) copy-start(bf16[4,128,1536]{2,1,0:T(8,128)(2,1)} %param.17) | copy-start | bytes 4718596
  794.8 156.8 %copy-start.121 = (f32[2,1536]{1,0:T(2,128)S(1)}, f32[2,1536]{1,0:T(2,128)}, u32[]{:S(2)}) copy-start(f32[2,1536]{1,0:T(2,128)} %copy-done.120) | copy-start | bytes 36868
  794.8 156.8 %copy-start.141 = (f32[1536]{0:T(1024)S(1)}, f32[1536]{0:T(1024)}, u32[]{:S(2)}) copy-start(f32[1536]{0:T(1024)} %copy-done.140) | copy-start | bytes 18436
  794.8 156.8 %copy-start.175 = (f32[128]{0:T(128)S(1)}, f32[128]{0:T(128)}, u32[]{:S(2)}) copy-start(f32[128]{0:T(128)} %copy-done.174) | copy-start | bytes 1540
  794.8 156.8 %copy-start.178 = (f32[128]{0:T(128)S(1)}, f32[128]{0:T(128)}, u32[]{:S(2)}) copy-start(f32[128]{0:T(128)} %copy-done.177) | copy-start | bytes 1540
  794.8 156.8 %copy-start.181 = (f32[128]{0:T(128)S(1)}, f32[128]{0:T(128)}, u32[]{:S(2)}) copy-start(f32[128]{0:T(128)} %copy-done.180) | copy-start | bytes 1540
  794.8 156.8 %copy-start.183 = (f32[128]{0:T(128)S(1)}, f32[128]{0:T(128)}, u32[]{:S(2)}) copy-start(f32[128]{0:T(128)} %copy-done.182) | copy-start | bytes 1540
  794.8 156.8 %copy-start.209 = (f32[128]{0:T(128)S(1)}, f32[128]{0:T(128)}, u32[]{:S(2)}) copy-start(f32[128]{0:T(128)} %copy-done.208) | copy-start | bytes 1540
  794.8 156.8 %copy-start.212 = (f32[128]{0:T(128)S(1)}, f32[128]{0:T(128)}, u32[]{:S(2)}) copy-start(f32[128]{0:T(128)} %copy-done.211) | copy-start | bytes 1540
  794.9 156.8 %copy-start.215 = (f32[128]{0:T(128)S(1)}, f32[128]{0:T(128)}, u32[]{:S(2)}) copy-start(f32[128]{0:T(128)} %copy-done.214) | copy-start | bytes 1540
  794.9 156.8 %copy-start.217 = (f32[128]{0:T(128)S(1)}, f32[128]{0:T(128)}, u32[]{:S(2)}) copy-start(f32[128]{0:T(128)} %copy-done.216) | copy-start | bytes 1540
  794.9 204.4 %all-reduce.17.cloned.1.call-start = ((), (), s32[]{:S(2)}) async-start(), calls=%async_computation.64 | async-start | bytes 393216 | tf_op jit(solution)/shard_map/psum | solution.py:292
  859.4 96.0 %copy-start.51 = (bf16[128,1536]{1,0:T(8,128)(2,1)S(1)}, bf16[128,1536]{1,0:T(8,128)(2,1)}, u32[]{:S(2)}) copy-start(bf16[128,1536]{1,0:T(8,128)(2,1)} %reduce-scatter.68.cloned.1.call-done) | copy-start | bytes 1179652
  963.4 98.8 %reduce-scatter.42.cloned.1.call-start = ((), (), s32[]{:S(2)}) async-start(), calls=%async_computation.41 | async-start | bytes 245760 | tf_op jit(solution)/shard_map/reduce_scatter | solution.py:122
  968.0 101.7 %reduce-scatter.34.cloned.1.call-start = ((), (), s32[]{:S(2)}) async-start(), calls=%async_computation.35 | async-start | bytes 245760 | tf_op jit(solution)/shard_map/reduce_scatter | solution.py:122
  972.7 98.7 %reduce-scatter.38.cloned.1.call-start = ((), (), s32[]{:S(2)}) async-start(), calls=%async_computation.38 | async-start | bytes 245760 | tf_op jit(solution)/shard_map/reduce_scatter | solution.py:122
  977.4 155.5 %reduce-scatter.84.cloned.1.call-start = ((), (), s32[]{:S(2)}) async-start(), calls=%async_computation.63 | async-start | bytes 884736
  1001.2 203.7 %reduce-scatter.78.cloned.1.call-start = ((), (), s32[]{:S(2)}) async-start(), calls=%async_computation.60 | async-start | bytes 2654208 | tf_op jit(solution)/shard_map/reduce_scatter | solution.py:288
  1003.5 273.5 %reduce-scatter.72.cloned.1.call-start = ((), (), s32[]{:S(2)}) async-start(), calls=%async_computation.57 | async-start | bytes 2654208 | tf_op jit(solution)/shard_map/reduce_scatter | solution.py:285
  1008.6 340.7 %reduce-scatter.74.cloned.1.call-start = ((), (), s32[]{:S(2)}) async-start(), calls=%async_computation.58 | async-start | bytes 2654208 | tf_op jit(solution)/shard_map/reduce_scatter | solution.py:286
  1018.5 402.9 %reduce-scatter.76.cloned.1.call-start = ((), (), s32[]{:S(2)}) async-start(), calls=%async_computation.59 | async-start | bytes 2654208 | tf_op jit(solution)/shard_map/reduce_scatter | solution.py:287
  1028.2 559.5 %reduce-scatter.82.cloned.1.call-start = ((), (), s32[]{:S(2)}) async-start(), calls=%async_computation.62 | async-start | bytes 10616832
  1048.3 706.0 %reduce-scatter.80.cloned.1.call-start = ((), (), s32[]{:S(2)}) async-start(), calls=%async_computation.61 | async-start | bytes 10616832 | tf_op jit(solution)/shard_map/reduce_scatter | solution.py:289
  (235 other events, 1875.5 us)
Sparse Core Ops, SparseCore 0:
  10.2 44.0 all-gather.19
  89.9 17.9 all-gather.31
  110.1 40.5 all-gather.21
  152.7 39.8 all-gather.17
  194.6 39.8 all-gather.23
  236.5 19.4 all-gather.15
  258.1 20.7 all-gather.29
  281.0 19.6 all-gather.33
  303.7 19.7 reduce-scatter.39
  325.5 79.8 all-gather.25
  407.6 78.0 all-gather.27
  488.6 17.8 reduce-scatter.43
  509.5 19.7 reduce-scatter.35
  532.1 19.7 reduce-scatter.31
  554.7 19.7 reduce-scatter.55
  597.7 19.7 reduce-scatter.57
  643.2 19.7 reduce-scatter.59
  665.8 19.7 reduce-scatter.51
  688.6 19.7 reduce-scatter.47
  711.2 19.7 reduce-scatter.45
  763.3 19.7 reduce-scatter.61
  786.1 19.7 reduce-scatter.53
  808.9 19.7 reduce-scatter.49
  831.1 28.1 reduce-scatter.67
  862.1 28.1 reduce-scatter.69
  892.6 28.1 reduce-scatter.65
  923.4 28.1 reduce-scatter.63
  963.5 35.7 all-reduce.16
  1002.4 19.8 reduce-scatter.41
  1024.7 19.7 reduce-scatter.33
  1047.1 19.7 reduce-scatter.37
  1070.5 62.4 reduce-scatter.83
  1136.9 67.9 reduce-scatter.77
  1209.0 67.9 reduce-scatter.71
  1281.1 68.1 reduce-scatter.73
  1353.2 68.1 reduce-scatter.75
  1425.3 162.3 reduce-scatter.81
  1591.9 162.4 reduce-scatter.79
where the time goes:
time: 1770 us; the launch traced here: 1760 us
  waiting for transfers between devices  1190 us (67%)
  blocking collectives  203 us (11%)
  matrix products  189 us (11%)
  local copies, waits for them, and re-layouts  87.4 us (5%)
  other arithmetic  72.9 us (4%)
  between operations  19.8 us (1%)
    unnamed x40, waiting for transfers between devices  185 us
    reduce_scatter x1, waiting for transfers between devices, on_device(): lax.psum_scatter(sum_up, 'item', scatter_dimension=0, tiled=True)  167 us
    reduce_scatter x4, waiting for transfers between devices, micro_step(): lax.psum_scatter(grad_joined[:media_count].astype(jnp.bfloat16), 'head',...  118 us
    reduce_scatter x4, waiting for transfers between devices, micro_step(): lax.psum_scatter(times_transposed(mixed, w_output).astype(jnp.bfloat16),...  78.4 us
    unnamed x2, blocking collectives  76.7 us
    all_gather x1, waiting for transfers between devices, on_device(): lax.all_gather(down_weight, 'item', axis=0, tiled=True)  76.2 us
    reduce_scatter x1, waiting for transfers between devices, on_device(): lax.psum_scatter(sum_key, 'item', scatter_dimension=0, tiled=True)  72.2 us
    reduce_scatter x1, waiting for transfers between devices, on_device(): lax.psum_scatter(sum_query, 'item', scatter_dimension=0, tiled=True)  72.1 us
  transfers between devices with their start and end apart: 38, of which 31 were waited for; matrix products, arithmetic and copies ran while one was open for 16% of the time, Pallas kernels for 0%

commit v1 on v0

v1 whole, which is shorter than its diff:
```python
import jax
import jax.numpy as jnp
from jax import lax
from jax.sharding import PartitionSpec as P

HEAD_DIM = 96
P_SIZE = 64
EPS = 1e-05
BF = jnp.bfloat16
F32 = jnp.float32


def norm_forward(rows, gain, bias):
    mean = jnp.mean(rows, axis=-1, keepdims=True)
    centered = rows - mean
    inverse = lax.rsqrt(jnp.mean(centered * centered, axis=-1, keepdims=True) + EPS)
    normed = centered * inverse
    return normed * gain + bias, normed, inverse


def norm_backward(upstream, normed, inverse, gain):
    scaled = upstream * gain
    first = jnp.mean(scaled, axis=-1, keepdims=True)
    second = jnp.mean(scaled * normed, axis=-1, keepdims=True)
    axes = tuple(range(upstream.ndim - 1))
    return (
        inverse * (scaled - first - normed * second),
        jnp.sum(upstream * normed, axis=axes),
        jnp.sum(upstream, axis=axes),
    )


def dot(left, right, a, b):
    return lax.dot_general(left, right, (((a,), (b,)), ((), ())), preferred_element_type=F32)


def gather_rows(rows):
    return lax.all_gather(rows, "head", axis=1, tiled=True)


def scatter_rows(rows):
    return lax.psum_scatter(rows.astype(BF), "head", scatter_dimension=1, tiled=True).astype(F32)


def item_scatter(grad):
    return lax.psum_scatter(grad.astype(BF), "item", scatter_dimension=0, tiled=True).astype(F32)


def on_device(
    media, latents, cotangent, frame_counts,
    query_weight, key_weight, value_weight, output_weight, up_weight, down_weight,
    media_gain, media_bias, latent_gain, latent_bias, ffn_gain, ffn_bias, time_embed,
):
    items, local_media, width = media.shape
    frames = time_embed.shape[0]
    local_frames = local_media // P_SIZE
    place = lax.axis_index("head")
    scale = HEAD_DIM ** (-0.5)
    small = jnp.concatenate(
        [jnp.stack([media_gain, media_bias, latent_gain, latent_bias, ffn_gain, ffn_bias]), time_embed]
    )
    small = lax.all_gather(small, "item", axis=1, tiled=True).astype(F32)
    g_media, b_media, g_latent, b_latent, g_ffn, b_ffn = (small[k] for k in range(6))
    time_rows = lax.dynamic_slice_in_dim(small[6:], place * local_frames, local_frames, 0)
    w_query, w_key, w_value, w_output, w_up, w_down = (
        lax.all_gather(w, "item", axis=0, tiled=True)
        for w in (query_weight, key_weight, value_weight, output_weight, up_weight, down_weight)
    )
    shifted = (
        media.astype(F32).reshape(items, local_frames, P_SIZE, width) + time_rows[None, :, None, :]
    ).reshape(media.shape)
    media_norm, media_hat, media_inv = norm_forward(shifted, g_media, b_media)
    latent_f = latents.astype(F32)
    latent_norm, latent_hat, latent_inv = norm_forward(latent_f, g_latent, b_latent)
    media_all = gather_rows(media_norm.astype(BF))
    latent_all = gather_rows(latent_norm.astype(BF))
    upstream = gather_rows(cotangent)
    media_count, latent_count = media_all.shape[1], latent_all.shape[1]
    joined = jnp.concatenate([media_all, latent_all], axis=1)
    key_count = joined.shape[1]
    local_heads = w_query.shape[1] // HEAD_DIM
    query = (scale * dot(latent_all, w_query, 2, 0)).astype(BF)
    keys = dot(joined, w_key, 2, 0).astype(BF)
    values = dot(joined, w_value, 2, 0).astype(BF)
    query_h = query.reshape(items, latent_count, local_heads, HEAD_DIM)
    key_h = keys.reshape(items, key_count, local_heads, HEAD_DIM)
    value_h = values.reshape(items, key_count, local_heads, HEAD_DIM)
    index = jnp.arange(key_count, dtype=jnp.int32)
    valid = (index[None, :] // P_SIZE < frame_counts[:, None]) | (index[None, :] >= media_count)
    valid = valid[:, None, None, :]

    def mix(spec, left, right):
        return jnp.einsum(spec, left, right, preferred_element_type=F32)

    scores = jnp.where(valid, mix("blhe,bnhe->bhln", query_h, key_h), -1e30)
    peak = jnp.max(scores, axis=-1, keepdims=True)
    expo = jnp.exp(scores - peak)
    weights = expo / jnp.sum(expo, axis=-1, keepdims=True)
    weights_low = weights.astype(BF)
    mixed = mix("bhln,bnhe->blhe", weights_low, value_h).reshape(items, latent_count, -1).astype(BF)
    middle = latent_f + scatter_rows(dot(mixed, w_output, 2, 1))
    ffn_norm, ffn_hat, ffn_inv = norm_forward(middle, g_ffn, b_ffn)
    ffn_all = gather_rows(ffn_norm.astype(BF))
    rows = items * latent_count
    ffn_rows = ffn_all.reshape(rows, width)
    up_rows = upstream.reshape(rows, width)
    pre = dot(ffn_rows, w_up, 1, 0)
    act, gelu_back = jax.vjp(jax.nn.gelu, pre)
    act = act.astype(BF)
    ffn_out = scatter_rows(dot(act, w_down, 1, 1).reshape(items, latent_count, width))
    output = (middle + ffn_out).astype(BF)
    grad_down = dot(up_rows, act, 0, 0)
    grad_pre = gelu_back(dot(up_rows, w_down, 1, 0))[0].astype(BF)
    grad_up = dot(ffn_rows, grad_pre, 0, 0)
    grad_ffn = scatter_rows(dot(grad_pre, w_up, 1, 1).reshape(items, latent_count, width))
    grad_mid, grad_fgain, grad_fbias = norm_backward(grad_ffn, ffn_hat, ffn_inv, g_ffn)
    grad_middle = cotangent.astype(F32) + grad_mid
    attended_grad = gather_rows(grad_middle.astype(BF)).reshape(rows, width)
    grad_output = dot(attended_grad, mixed.reshape(rows, -1), 0, 0)
    grad_mixed = dot(attended_grad, w_output, 1, 0).astype(BF)
    gm_h = grad_mixed.reshape(items, latent_count, local_heads, HEAD_DIM)
    grad_values = mix("bhln,blhe->bnhe", weights_low, gm_h).astype(BF).reshape(items * key_count, -1)
    grad_weights = mix("blhe,bnhe->bhln", gm_h, value_h)
    inner = jnp.sum(weights * grad_weights, axis=-1, keepdims=True)
    grad_scores = (weights * (grad_weights - inner)).astype(BF)
    grad_query = mix("bhln,bnhe->blhe", grad_scores, key_h).astype(BF).reshape(rows, -1)
    grad_keys = mix("bhln,blhe->bnhe", grad_scores, query_h).astype(BF).reshape(items * key_count, -1)
    joined_rows = joined.reshape(items * key_count, width)
    grad_wquery = scale * dot(latent_all.reshape(rows, width), grad_query, 0, 0)
    grad_wkey = dot(joined_rows, grad_keys, 0, 0)
    grad_wvalue = dot(joined_rows, grad_values, 0, 0)
    grad_joined = dot(grad_keys, w_key, 1, 1) + dot(grad_values, w_value, 1, 1)
    grad_joined = grad_joined.reshape(items, key_count, width)
    grad_latent_all = grad_joined[:, media_count:] + scale * dot(grad_query, w_query, 1, 1).reshape(
        items, latent_count, width
    )
    media_back = scatter_rows(grad_joined[:, :media_count])
    latent_back = scatter_rows(grad_latent_all)
    grad_media, grad_mgain, grad_mbias = norm_backward(media_back, media_hat, media_inv, g_media)
    grad_lat, grad_lgain, grad_lbias = norm_backward(latent_back, latent_hat, latent_inv, g_latent)
    time_local = jnp.sum(grad_media.reshape(items, local_frames, P_SIZE, width), axis=(0, 2))
    grad_time = lax.dynamic_update_slice_in_dim(
        jnp.zeros((frames, width), F32), time_local, place * local_frames, 0
    )
    smalls = jnp.concatenate(
        [jnp.stack([grad_mgain, grad_mbias, grad_lgain, grad_lbias, grad_fgain, grad_fbias]), grad_time]
    )
    smalls = lax.psum_scatter(smalls, ("item",), scatter_dimension=1, tiled=True)
    smalls = lax.psum(smalls, "head")
    return (
        output,
        grad_middle + grad_lat,
        grad_media,
        *(item_scatter(g) for g in (grad_wquery, grad_wkey, grad_wvalue, grad_output, grad_up, grad_down)),
        *(smalls[k] for k in range(6)),
        smalls[6:],
    )


def solution(mesh):
    rows = P("item", "head", None)
    block = P("item", "head")
    vector = P("item")
    table = P(None, "item")
    return jax.shard_map(
        on_device,
        mesh=mesh,
        in_specs=(rows,) * 3 + (vector,) + (block,) * 6 + (vector,) * 6 + (table,),
        out_specs=(rows,) * 3 + (block,) * 6 + (vector,) * 6 + (table,),
        check_vma=False,
    )
```

time: 1770 us -> 1170 us (0.66)
  waiting for transfers between devices: 1190 us -> 874 us
  blocking collectives: 203 us -> 77.4 us
  matrix products: 189 us -> 102 us
  other arithmetic: 72.9 us -> 29.8 us
  local copies, waits for them, and re-layouts: 87.4 us -> 69.3 us
    reduce_scatter x25 -> x10, waiting for transfers between devices: 753 us -> 444 us  [the longest x5 359 us: item_scatter(): lax.psum_scatter(grad.astype(BF), 'item', scatter_dimension=0, tiled=True)]
    dot_general x96 -> x24, matrix products: 189 us -> 102 us  [the longest x18 91.8 us: dot(): lax.dot_general(left, right, (((a,), (b,)), ((), ())), preferred_element_...]
    unnamed x2 -> x0, blocking collectives: 76.7 us -> none
    all_gather x17 -> x5, blocking collectives: 127 us -> 67.3 us  [the longest x4 34.8 us: gather_rows(): return lax.all_gather(rows, 'head', axis=1, tiled=True)]
    all_gather x10 -> x7, waiting for transfers between devices: 230 us -> 265 us  [the longest x6 229 us: on_device(): lax.all_gather(w, 'item', axis=0, tiled=True)]
    unnamed x548 -> x106, local copies, waits for them, and re-layouts: 50.7 us -> 21.6 us
    reduce_sum x29 -> x11, other arithmetic: 32.9 us -> 12.3 us  [the longest x3 6.26 us: norm_backward(): jnp.sum(upstream * normed, axis=axes)]
    unnamed x40 -> x21, waiting for transfers between devices: 185 us -> 164 us
  transfers between devices with their start and end apart: 38 -> 19, of which waited for: 31 -> 17; matrix products, arithmetic and copies ran while one was open for 16% -> 12% of each run, Pallas kernels for 0% -> 0%
where the time goes in v1:
time: 1170 us
  waiting for transfers between devices  874 us (75%)
  matrix products  102 us (9%)
  blocking collectives  77.4 us (7%)
  local copies, waits for them, and re-layouts  69.3 us (6%)
  other arithmetic  29.8 us (3%)
  between operations  14.8 us (1%)
    reduce_scatter x5, waiting for transfers between devices, item_scatter(): lax.psum_scatter(grad.astype(BF), 'item', scatter_dimension=0, tiled=True)  359 us
    all_gather x6, waiting for transfers between devices, on_device(): lax.all_gather(w, 'item', axis=0, tiled=True)  229 us
    unnamed x21, waiting for transfers between devices  164 us
    dot_general x18, matrix products, dot(): lax.dot_general(left, right, (((a,), (b,)), ((), ())), preferred_element_...  91.8 us
    reduce_scatter x5, waiting for transfers between devices, scatter_rows(): lax.psum_scatter(rows.astype(BF), 'head', scatter_dimension=1, tiled=True)  85.4 us
    all_gather x1, waiting for transfers between devices, gather_rows(): return lax.all_gather(rows, 'head', axis=1, tiled=True)  35.8 us
    all_gather x4, blocking collectives, gather_rows(): return lax.all_gather(rows, 'head', axis=1, tiled=True)  34.8 us
    all_gather x1, blocking collectives, on_device(): small = lax.all_gather(small, 'item', axis=1, tiled=True).astype(F32)  32.5 us
  transfers between devices with their start and end apart: 19, of which 17 were waited for; matrix products, arithmetic and copies ran while one was open for 12% of the time, Pallas kernels for 0%

profile of v1, /device:TPU:0, one launch (start us, length us, event | category | flops | bytes accessed | tf_op | source)
XLA Modules:
  0.0 1168.4 jit_solution(14356322088055814597)
XLA Ops:
  12.7 32.5 %all-gather = bf16[8,192,14]{1,2,0:T(8,128)(2,1)S(1)} all-gather(bf16[1,192,14]{1,2,0:T(8,128)(2,1)S(1)} %bitcast.120), channel_id=1, replica_groups=mesh['item'=8,'head'=4] {'item'}, dimensions={0}, use_global_device_ids=true | all-gather | bytes 48384 | tf_op jit(solution)/shard_map/all_gather | solution.py:62
  47.7 1.9 add_convert_fusion
  53.3 9.2 all_gather.38
  62.5 2.2 fusion.33
  65.6 35.8 %all-gather.9.cloned.1.call-done = bf16[4,512,1536]{2,1,0:T(8,128)(2,1)} async-done(((bf16[4,128,1536]{2,1,0:T(8,128)(2,1)}), bf16[4,512,1536]{2,1,0:T(8,128)(2,1)}) %all-gather.9.cloned.1.call-update) | async-done | bytes 6291472 | tf_op jit(solution)/shard_map/all_gather | solution.py:38
  101.4 5.8 constant_dynamic-update-slice_fusion.1
  108.2 36.5 %all-gather.15.cloned.1.call-done = bf16[1536,384]{1,0:T(8,128)(2,1)} async-done(((bf16[192,384]{1,0:T(8,128)(2,1)}), bf16[1536,384]{1,0:T(8,128)(2,1)}) %all-gather.15.cloned.1.call-update) | async-done | bytes 1179664 | tf_op jit(solution)/shard_map/all_gather | solution.py:66
  144.7 8.3 convolution_convert_fusion.7
  153.0 3.9 copy.83
  156.9 29.7 %all-gather.11.cloned.1.call-done = bf16[1536,384]{1,0:T(8,128)(2,1)} async-done(((bf16[192,384]{1,0:T(8,128)(2,1)}), bf16[1536,384]{1,0:T(8,128)(2,1)}) %all-gather.11.cloned.1.call-update) | async-done | bytes 1179664 | tf_op jit(solution)/shard_map/all_gather | solution.py:66
  186.6 8.3 convolution_convert_fusion.8
  194.9 3.9 copy.82
  198.9 2.1 fusion.68
  204.0 24.5 %all-gather.17.cloned.1.call-done = bf16[1536,384]{1,0:T(8,128)(2,1)} async-done(((bf16[192,384]{1,0:T(8,128)(2,1)}), bf16[1536,384]{1,0:T(8,128)(2,1)}) %all-gather.17.cloned.1.call-update) | async-done | bytes 1179664 | tf_op jit(solution)/shard_map/all_gather | solution.py:66
  228.5 2.8 convolution_convert_fusion.4
  232.1 9.0 all_gather.46
  241.1 68.1 %all-gather.21.cloned.1.call-done = bf16[1536,1536]{1,0:T(8,128)(2,1)} async-done(((bf16[192,1536]{1,0:T(8,128)(2,1)}), bf16[1536,1536]{1,0:T(8,128)(2,1)}) %all-gather.21.cloned.1.call-update) | async-done | bytes 4718608 | tf_op jit(solution)/shard_map/all_gather | solution.py:66
  309.2 5.1 fusion.79
  314.4 19.4 %reduce-scatter.17.cloned.1.call-done = bf16[4,16,1536]{2,1,0:T(8,128)(2,1)} async-done(((bf16[4,64,1536]{2,1,0:T(8,128)(2,1)}), bf16[4,16,1536]{2,1,0:T(8,128)(2,1)}) %reduce-scatter.17.cloned.1.call-update) | async-done | bytes 196624 | tf_op jit(solution)/shard_map/reduce_scatter | solution.py:42
  337.1 8.4 all_gather.43
  345.4 70.7 %all-gather.19.cloned.1.call-done = bf16[1536,1536]{1,0:T(8,128)(2,1)} async-done(((bf16[192,1536]{1,0:T(8,128)(2,1)}), bf16[1536,1536]{1,0:T(8,128)(2,1)}) %all-gather.19.cloned.1.call-update) | async-done | bytes 4718608 | tf_op jit(solution)/shard_map/all_gather | solution.py:66
  416.1 6.2 fusion.25
  422.3 2.3 convolution_convert_fusion.5
  424.7 21.5 %reduce-scatter.21.cloned.1.call-done = bf16[4,16,1536]{2,1,0:T(8,128)(2,1)} async-done(((bf16[4,64,1536]{2,1,0:T(8,128)(2,1)}), bf16[4,16,1536]{2,1,0:T(8,128)(2,1)}) %reduce-scatter.21.cloned.1.call-update) | async-done | bytes 196624 | tf_op jit(solution)/shard_map/reduce_scatter | solution.py:42
  446.2 1.9 fusion.61
  450.0 8.2 all_gather.47
  460.3 1.8 reshape.239
  462.1 3.2 multiply_reduce_fusion.1
  468.6 2.0 convert_bitcast_fusion.1
  471.5 2.8 copy.90
  474.3 4.6 reshape.241
  478.9 1.9 dot_general.91
  480.7 4.3 copy.88
  485.1 4.4 reshape.240
  489.5 5.9 fusion.80
  495.4 7.4 convolution_add_fusion
  502.8 2.9 fusion.15
  505.8 8.0 slice.89
  513.9 5.3 convolution_convert_fusion.6
  519.7 1.9 reshape.244
  521.5 2.9 fusion.12
  524.5 2.8 fusion.13
  527.3 8.4 convolution_convert_fusion.3
  535.8 9.5 convolution_convert_fusion.2
  545.4 5.5 fusion.1
  550.9 6.7 copy.94
  557.9 4.7 convolution_convert_fusion.1
  564.6 26.1 %reduce-scatter.25.cloned.1.call-done = bf16[4,128,1536]{2,1,0:T(8,128)(2,1)} async-done(((bf16[4,512,1536]{2,1,0:T(8,128)(2,1)}), bf16[4,128,1536]{2,1,0:T(8,128)(2,1)}) %reduce-scatter.25.cloned.1.call-update) | async-done | bytes 1572880 | tf_op jit(solution)/shard_map/reduce_scatter | solution.py:42
  590.7 3.2 fusion.8
  594.0 2.5 fusion.75
  598.0 18.4 %reduce-scatter.19.cloned.1.call-done = bf16[4,16,1536]{2,1,0:T(8,128)(2,1)} async-done(((bf16[4,64,1536]{2,1,0:T(8,128)(2,1)}), bf16[4,16,1536]{2,1,0:T(8,128)(2,1)}) %reduce-scatter.19.cloned.1.call-update) | async-done | bytes 196624 | tf_op jit(solution)/shard_map/reduce_scatter | solution.py:42
  616.4 2.1 fusion.54
  618.5 66.3 %reduce-scatter.27.cloned.1.call-done = bf16[192,384]{1,0:T(8,128)(2,1)} async-done(((bf16[1536,384]{1,0:T(8,128)(2,1)}), bf16[192,384]{1,0:T(8,128)(2,1)}) %reduce-scatter.27.cloned.1.call-update) | async-done | bytes 147472 | tf_op jit(solution)/shard_map/reduce_scatter | solution.py:46
  684.8 1.6 convert_element_type.189
  686.5 65.1 %reduce-scatter.33.cloned.1.call-done = bf16[192,384]{1,0:T(8,128)(2,1)} async-done(((bf16[1536,384]{1,0:T(8,128)(2,1)}), bf16[192,384]{1,0:T(8,128)(2,1)}) %reduce-scatter.33.cloned.1.call-update) | async-done | bytes 147472 | tf_op jit(solution)/shard_map/reduce_scatter | solution.py:46
  751.6 1.6 convert_element_type.195
  753.2 65.8 %reduce-scatter.29.cloned.1.call-done = bf16[192,384]{1,0:T(8,128)(2,1)} async-done(((bf16[1536,384]{1,0:T(8,128)(2,1)}), bf16[192,384]{1,0:T(8,128)(2,1)}) %reduce-scatter.29.cloned.1.call-update) | async-done | bytes 147472 | tf_op jit(solution)/shard_map/reduce_scatter | solution.py:46
  819.0 1.6 convert_element_type.191
  820.6 65.2 %reduce-scatter.31.cloned.1.call-done = bf16[192,384]{1,0:T(8,128)(2,1)} async-done(((bf16[1536,384]{1,0:T(8,128)(2,1)}), bf16[192,384]{1,0:T(8,128)(2,1)}) %reduce-scatter.31.cloned.1.call-update) | async-done | bytes 147472 | tf_op jit(solution)/shard_map/reduce_scatter | solution.py:46
  887.5 96.9 %reduce-scatter.37.cloned.1.call-done = bf16[192,1536]{1,0:T(8,128)(2,1)} async-done(((bf16[1536,1536]{1,0:T(8,128)(2,1)}), bf16[192,1536]{1,0:T(8,128)(2,1)}) %reduce-scatter.37.cloned.1.call-update) | async-done | bytes 589840
  987.0 96.5 %reduce-scatter.35.cloned.1.call-done = bf16[192,1536]{1,0:T(8,128)(2,1)} async-done(((bf16[1536,1536]{1,0:T(8,128)(2,1)}), bf16[192,1536]{1,0:T(8,128)(2,1)}) %reduce-scatter.35.cloned.1.call-update) | async-done | bytes 589840 | tf_op jit(solution)/shard_map/reduce_scatter | solution.py:46
  1083.6 2.2 convert_element_type.197
  1085.8 63.7 %reduce-scatter.39.cloned.1.call-done = f32[192,14]{1,0:T(8,128)} async-done(((f32[1536,14]{1,0:T(8,128)}), f32[192,14]{1,0:T(8,128)}) %reduce-scatter.39.cloned.1.call-update) | async-done | bytes 10768
  1150.4 10.1 psum.7
  (205 shorter events, 39.6 us)
Async XLA Ops:
  7.2 38.9 %copy-start = (bf16[4,128,1536]{2,1,0:T(8,128)(2,1)S(1)}, bf16[4,128,1536]{2,1,0:T(8,128)(2,1)}, u32[]{:S(2)}) copy-start(bf16[4,128,1536]{2,1,0:T(8,128)(2,1)} %param.17) | copy-start | bytes 4718596
  7.2 55.3 %all-gather.13.cloned.1.call-start = ((), (), s32[]{:S(2)}) async-start(), calls=%async_computation.14 | async-start | bytes 1327104 | tf_op jit(solution)/shard_map/all_gather | solution.py:66
  7.9 93.5 %all-gather.9.cloned.1.call-start = ((), (), s32[]{:S(2)}) async-start(), calls=%async_computation.12 | async-start | bytes 7864320 | tf_op jit(solution)/shard_map/all_gather | solution.py:38
  46.0 1.1 copy-start.24
  49.6 2.6 copy-start.1
  49.6 2.9 copy-start.48
  49.6 95.1 %all-gather.15.cloned.1.call-start = ((), (), s32[]{:S(2)}) async-start(), calls=%async_computation.15 | async-start | bytes 1327104 | tf_op jit(solution)/shard_map/all_gather | solution.py:66
  50.4 136.2 %all-gather.11.cloned.1.call-start = ((), (), s32[]{:S(2)}) async-start(), calls=%async_computation.13 | async-start | bytes 1327104 | tf_op jit(solution)/shard_map/all_gather | solution.py:66
  50.9 177.6 %all-gather.17.cloned.1.call-start = ((), (), s32[]{:S(2)}) async-start(), calls=%async_computation.16 | async-start | bytes 1327104 | tf_op jit(solution)/shard_map/all_gather | solution.py:66
  51.5 257.7 %all-gather.21.cloned.1.call-start = ((), (), s32[]{:S(2)}) async-start(), calls=%async_computation.19 | async-start | bytes 5308416 | tf_op jit(solution)/shard_map/all_gather | solution.py:66
  52.1 281.7 %reduce-scatter.17.cloned.1.call-start = ((), (), s32[]{:S(2)}) async-start(), calls=%async_computation.17 | async-start | bytes 983040 | tf_op jit(solution)/shard_map/reduce_scatter | solution.py:42
  52.3 0.9 copy-start.30
  62.5 44.7 %copy-start.8 = (bf16[4,64,1536]{2,1,0:T(8,128)(2,1)}, bf16[4,64,1536]{2,1,0:T(8,128)(2,1)S(1)}, u32[]{:S(2)}) copy-start(bf16[4,64,1536]{2,1,0:T(8,128)(2,1)S(1)} %all_gather.38) | copy-start | bytes 2359300
  194.9 3.9 copy-start.9
  198.9 2.1 copy-start.47
  200.9 1.5 copy-start.11
  202.1 1.5 copy-start.4
  202.1 1.5 copy-start.34
  203.8 28.3 %copy-start.13 = (bf16[4,16,1536]{2,1,0:T(8,128)(2,1)S(1)}, bf16[4,16,1536]{2,1,0:T(8,128)(2,1)}, u32[]{:S(2)}) copy-start(bf16[4,16,1536]{2,1,0:T(8,128)(2,1)} %param.19) | copy-start | bytes 589828
  204.0 37.1 %copy-start.20 = (bf16[4,64,384]{2,1,0:T(8,128)(2,1)}, bf16[4,64,384]{2,1,0:T(8,128)(2,1)S(1)}, u32[]{:S(2)}) copy-start(bf16[4,64,384]{2,1,0:T(8,128)(2,1)S(1)} %convert_element_type.162) | copy-start | bytes 589828
  231.3 184.8 %all-gather.19.cloned.1.call-start = ((), (), s32[]{:S(2)}) async-start(), calls=%async_computation.18 | async-start | bytes 5308416 | tf_op jit(solution)/shard_map/all_gather | solution.py:66
  232.0 214.2 %reduce-scatter.21.cloned.1.call-start = ((), (), s32[]{:S(2)}) async-start(), calls=%async_computation.21 | async-start | bytes 983040 | tf_op jit(solution)/shard_map/reduce_scatter | solution.py:42
  309.2 26.8 %copy-start.38 = (f32[1536]{0:T(1024)S(1)}, f32[1536]{0:T(1024)}, u32[]{:S(2)}) copy-start(f32[1536]{0:T(1024)} %get-tuple-element.109) | copy-start | bytes 18436
  334.8 1.2 copy-start.26
  335.9 1.1 copy-start.28
  416.1 6.2 copy-start.49
  422.3 2.3 copy-start.19
  422.3 23.9 %copy-start.6 = (bf16[4,16,1536]{2,1,0:T(8,128)(2,1)S(1)}, bf16[4,16,1536]{2,1,0:T(8,128)(2,1)}, u32[]{:S(2)}) copy-start(bf16[4,16,1536]{2,1,0:T(8,128)(2,1)} %reduce-scatter.17.cloned.1.call-done) | copy-start | bytes 589828
  424.7 138.7 %reduce-scatter.23.cloned.1.call-start = ((), (), s32[]{:S(2)}) async-start(), calls=%async_computation.22 | async-start | bytes 983040 | tf_op jit(solution)/shard_map/reduce_scatter | solution.py:42
  446.2 12.8 %copy-start.17 = (bf16[1536,384]{1,0:T(8,128)(2,1)S(1)}, bf16[1536,384]{1,0:T(8,128)(2,1)}, u32[]{:S(2)}) copy-start(bf16[1536,384]{1,0:T(8,128)(2,1)} %all-gather.17.cloned.1.call-done) | copy-start | bytes 3538948
  458.2 0.9 copy-start.22
  462.1 3.2 copy-start.5
  462.1 3.2 copy-start.23
  462.1 3.2 copy-start.35
  466.1 1.5 copy-start.2
  467.6 0.9 copy-start.10
  489.5 5.9 copy-start.3
  489.5 5.9 copy-start.15
  495.4 7.4 copy-start.16
  495.4 7.4 copy-start.18
  505.8 84.9 %reduce-scatter.25.cloned.1.call-start = ((), (), s32[]{:S(2)}) async-start(), calls=%async_computation.23 | async-start | bytes 7864320 | tf_op jit(solution)/shard_map/reduce_scatter | solution.py:42
  513.9 102.5 %reduce-scatter.19.cloned.1.call-start = ((), (), s32[]{:S(2)}) async-start(), calls=%async_computation.20 | async-start | bytes 983040 | tf_op jit(solution)/shard_map/reduce_scatter | solution.py:42
  519.2 165.6 %reduce-scatter.27.cloned.1.call-start = ((), (), s32[]{:S(2)}) async-start(), calls=%async_computation.24 | async-start | bytes 1327104 | tf_op jit(solution)/shard_map/reduce_scatter | solution.py:46
  524.4 227.1 %reduce-scatter.33.cloned.1.call-start = ((), (), s32[]{:S(2)}) async-start(), calls=%async_computation.27 | async-start | bytes 1327104 | tf_op jit(solution)/shard_map/reduce_scatter | solution.py:46
  527.3 291.7 %reduce-scatter.29.cloned.1.call-start = ((), (), s32[]{:S(2)}) async-start(), calls=%async_computation.25 | async-start | bytes 1327104 | tf_op jit(solution)/shard_map/reduce_scatter | solution.py:46
  535.8 350.0 %reduce-scatter.31.cloned.1.call-start = ((), (), s32[]{:S(2)}) async-start(), calls=%async_computation.26 | async-start | bytes 1327104 | tf_op jit(solution)/shard_map/reduce_scatter | solution.py:46
  545.4 439.1 %reduce-scatter.37.cloned.1.call-start = ((), (), s32[]{:S(2)}) async-start(), calls=%async_computation.29 | async-start | bytes 5308416
  557.6 525.9 %reduce-scatter.35.cloned.1.call-start = ((), (), s32[]{:S(2)}) async-start(), calls=%async_computation.28 | async-start | bytes 5308416 | tf_op jit(solution)/shard_map/reduce_scatter | solution.py:46
  562.6 0.7 copy-start.37
  562.6 0.7 copy-start.36
  562.6 0.8 copy-start.31
  562.6 0.8 copy-start.40
  562.6 28.1 %copy-start.25 = (f32[1536]{0:T(1024)S(1)}, f32[1536]{0:T(1024)}, u32[]{:S(2)}) copy-start(f32[1536]{0:T(1024)} %copy-done.24) | copy-start | bytes 18436
  562.6 28.1 %copy-start.33 = (f32[4,128]{1,0:T(4,128)S(1)}, f32[4,128]{1,0:T(4,128)}, u32[]{:S(2)}) copy-start(f32[4,128]{1,0:T(4,128)} %copy-done.32) | copy-start | bytes 6148
  562.6 28.1 %copy-start.42 = (f32[4,128]{1,0:T(4,128)S(1)}, f32[4,128]{1,0:T(4,128)}, u32[]{:S(2)}) copy-start(f32[4,128]{1,0:T(4,128)} %copy-done.41) | copy-start | bytes 6148
  562.7 586.8 %reduce-scatter.39.cloned.1.call-start = ((), (), s32[]{:S(2)}) async-start(), calls=%async_computation.30 | async-start | bytes 884736
  590.7 3.2 copy-start.7
  596.5 19.9 %copy-start.12 = (bf16[4,16,1536]{2,1,0:T(8,128)(2,1)S(1)}, bf16[4,16,1536]{2,1,0:T(8,128)(2,1)}, u32[]{:S(2)}) copy-start(bf16[4,16,1536]{2,1,0:T(8,128)(2,1)} %reduce-scatter.21.cloned.1.call-done) | copy-start | bytes 589828
  596.5 19.9 %copy-start.14 = (bf16[4,16,1536]{2,1,0:T(8,128)(2,1)S(1)}, bf16[4,16,1536]{2,1,0:T(8,128)(2,1)}, u32[]{:S(2)}) copy-start(bf16[4,16,1536]{2,1,0:T(8,128)(2,1)} %param.19) | copy-start | bytes 589828
  596.5 19.9 %copy-start.21 = (bf16[4,16,1536]{2,1,0:T(8,128)(2,1)S(1)}, bf16[4,16,1536]{2,1,0:T(8,128)(2,1)}, u32[]{:S(2)}) copy-start(bf16[4,16,1536]{2,1,0:T(8,128)(2,1)} %reduce-scatter.23.cloned.1.call-done) | copy-start | bytes 589828
  596.5 19.9 %copy-start.27 = (f32[4,16]{1,0:T(4,128)S(1)}, f32[4,16]{1,0:T(4,128)}, u32[]{:S(2)}) copy-start(f32[4,16]{1,0:T(4,128)} %copy-done.26) | copy-start | bytes 772
  596.5 19.9 %copy-start.29 = (f32[4,16]{1,0:T(4,128)S(1)}, f32[4,16]{1,0:T(4,128)}, u32[]{:S(2)}) copy-start(f32[4,16]{1,0:T(4,128)} %copy-done.28) | copy-start | bytes 772
  596.5 19.9 %copy-start.44 = (f32[4,16]{1,0:T(4,128)S(1)}, f32[4,16]{1,0:T(4,128)}, u32[]{:S(2)}) copy-start(f32[4,16]{1,0:T(4,128)} %copy-done.43) | copy-start | bytes 772
  596.5 19.9 %copy-start.46 = (f32[4,16]{1,0:T(4,128)S(1)}, f32[4,16]{1,0:T(4,128)}, u32[]{:S(2)}) copy-start(f32[4,16]{1,0:T(4,128)} %copy-done.45) | copy-start | bytes 772
  (5 other events, 3.1 us)
Sparse Core Ops, SparseCore 0:
  10.2 43.8 all-gather.12
  56.3 45.1 all-gather.8
  103.6 41.0 all-gather.14
  146.7 39.8 all-gather.10
  188.6 39.8 all-gather.16
  230.5 78.6 all-gather.20
  312.3 21.3 reduce-scatter.16
  336.2 79.8 all-gather.18
  424.8 21.4 reduce-scatter.20
  505.9 23.6 reduce-scatter.22
  532.3 58.3 reduce-scatter.24
  593.1 23.2 reduce-scatter.18
  620.7 64.0 reduce-scatter.26
  688.5 63.0 reduce-scatter.32
  755.8 63.1 reduce-scatter.28
  822.6 63.1 reduce-scatter.30
  889.8 94.5 reduce-scatter.36
  988.4 95.1 reduce-scatter.34
  1087.2 62.1 reduce-scatter.38
